TPU v7x, 256 devices: a whole 4x4x8 slice. The times are simulated.
256 devices in a mesh: ctx: 64 (over x, z, y_hi), tp: 4 (over y_lo, core).
Axes of the slice: x: 4, y: 4 (y_hi: 2, y_lo: 2; y = y_hi * 2 + y_lo), z: 8, core: 2. Of those that a mesh axis runs over, the one named last changes fastest.
Arguments:
- queries: bfloat16 [65536, 2048], P('ctx', 'tp'), may hold values from -6 to 6
- keys: bfloat16 [65536, 2048], P('ctx', 'tp'), may hold values from -6 to 6
- values: bfloat16 [65536, 2048], P('ctx', 'tp'), may hold values from -6 to 6
- offsets: int32 [32, 2], replicated, may hold values from 0 to 15
- out_weight: bfloat16 [2048, 2048], P('tp'), may hold values from -0.125 to 0.125
Outputs:
- mixed: bfloat16 [65536, 2048], P(('ctx', 'tp'))
All inputs are finite; a program needn't handle non-finite values.
Results may differ from a plain program's by a relative error of at most 0.015.
Values may be sent and summed in bfloat16 or wider, within the bound.
No kernel may reach another device: no remote copies, remote signals or barrier semaphores. Data moves between devices by JAX's collectives and lax.ppermute only.
A program may use at most 128 MiB of HBM per device.

v0:
```python
import jax
import jax.numpy as jnp
from jax import lax
from jax.sharding import PartitionSpec as P

HEAD_DIM = 64
SECOND_DILATION = 8
SPAN_BITS = 3
THIRD_DILATION = 16
NEG = -1e30


def partner_2(shard, axis, stride):
    return lax.ppermute(shard, axis, [(i, i ^ 1 << stride) for i in range(lax.axis_size(axis))])


def select_rows(field, dilation, start_offset, heads_on_shard):
    count_of_rows = field.shape[0]
    shaped = field.reshape(count_of_rows // dilation, dilation, heads_on_shard, HEAD_DIM)
    picked = lax.broadcasted_iota(
        jnp.int32, (1, dilation, heads_on_shard, 1), 1
    ) == start_offset.reshape(1, 1, heads_on_shard, 1)
    return jnp.sum(jnp.where(picked, shaped, jnp.zeros_like(shaped)), axis=1)


def attend(inputs):
    query_per_head, key_per_head, value_per_head = inputs
    scores = jnp.dot(
        query_per_head, key_per_head.T, preferred_element_type=jnp.float32
    ) * HEAD_DIM ** (-0.5)
    peak = jnp.max(scores, axis=1)
    expo = jnp.exp(scores - peak[:, None])
    total = jnp.sum(expo, axis=1)
    summed = jnp.dot(expo.astype(jnp.bfloat16), value_per_head, preferred_element_type=jnp.float32)
    return (peak, total, summed)


def widen_pattern(peak, total, summed, dilation, start_offset, count_of_rows):
    heads_on_shard = peak.shape[0]
    hit = lax.broadcasted_iota(jnp.int32, (1, 1, dilation), 2) == start_offset.reshape(
        heads_on_shard, 1, 1
    )
    peak_full = jnp.where(hit, peak[:, :, None], NEG).reshape(heads_on_shard, count_of_rows)
    total_full = jnp.where(hit, total[:, :, None], 0.0).reshape(heads_on_shard, count_of_rows)
    summed_full = jnp.where(hit[:, :, :, None], summed[:, :, None, :], 0.0).reshape(
        heads_on_shard, count_of_rows, HEAD_DIM
    )
    return (peak_full, total_full, summed_full)


def local(queries, keys, values, offsets, out_weight):
    count_of_rows = queries.shape[0]
    heads_on_shard = queries.shape[1] // HEAD_DIM
    segment_width = heads_on_shard * HEAD_DIM
    shard_offsets = lax.dynamic_slice_in_dim(
        offsets, lax.axis_index("tp") * heads_on_shard, heads_on_shard, 0
    )
    nearby_offset = shard_offsets[:, 0] % SECOND_DILATION
    distant_offset = shard_offsets[:, 1] % THIRD_DILATION

    def heads_first(field):
        return field.reshape(field.shape[0], heads_on_shard, HEAD_DIM).transpose(1, 0, 2)

    local_parts = lax.map(attend, (heads_first(queries), heads_first(keys), heads_first(values)))
    nearby_query = select_rows(queries, SECOND_DILATION, nearby_offset, heads_on_shard)
    near_kv = jnp.stack(
        [
            select_rows(keys, SECOND_DILATION, nearby_offset, heads_on_shard).reshape(
                -1, segment_width
            ),
            select_rows(values, SECOND_DILATION, nearby_offset, heads_on_shard).reshape(
                -1, segment_width
            ),
        ]
    )
    for bit in range(SPAN_BITS):
        partner = partner_2(near_kv, "ctx", bit)
        near_kv = jnp.concatenate([near_kv, partner], axis=1)
    nearby_partials = lax.map(
        attend, (nearby_query.transpose(1, 0, 2), heads_first(near_kv[0]), heads_first(near_kv[1]))
    )
    nearby_partials = widen_pattern(
        nearby_partials[0],
        nearby_partials[1],
        nearby_partials[2],
        SECOND_DILATION,
        nearby_offset,
        count_of_rows,
    )
    distant_query = select_rows(queries, THIRD_DILATION, distant_offset, heads_on_shard).transpose(
        1, 0, 2
    )
    far_kv = jnp.stack(
        [
            select_rows(keys, THIRD_DILATION, distant_offset, heads_on_shard).reshape(
                -1, segment_width
            ),
            select_rows(values, THIRD_DILATION, distant_offset, heads_on_shard).reshape(
                -1, segment_width
            ),
        ]
    )
    far_rows = distant_query.shape[1]
    piece = lax.all_gather(far_kv, "ctx", axis=1, tiled=True)
    fold_peak = jnp.full((heads_on_shard, far_rows), NEG, jnp.float32)
    piece_k = heads_first(piece[0])
    piece_v = heads_first(piece[1])
    scores = jnp.einsum(
        "hld,hsd->hls", distant_query, piece_k, preferred_element_type=jnp.float32
    ) * HEAD_DIM ** (-0.5)
    new_peak = jnp.maximum(fold_peak, jnp.max(scores, axis=2))
    expo = jnp.exp(scores - new_peak[:, :, None])
    fold_total = jnp.sum(expo, axis=2)
    fold_summed = jnp.einsum(
        "hls,hsd->hld", expo.astype(jnp.bfloat16), piece_v, preferred_element_type=jnp.float32
    )
    distant_partials = (new_peak, fold_total, fold_summed)
    distant_partials = widen_pattern(
        distant_partials[0],
        distant_partials[1],
        distant_partials[2],
        THIRD_DILATION,
        distant_offset,
        count_of_rows,
    )
    parts = [local_parts, nearby_partials, distant_partials]
    top = jnp.maximum(jnp.maximum(parts[0][0], parts[1][0]), parts[2][0])
    numer = jnp.zeros((heads_on_shard, count_of_rows, HEAD_DIM), jnp.float32)
    denom = jnp.zeros((heads_on_shard, count_of_rows), jnp.float32)
    for peak, total, summed in parts:
        factor = jnp.exp(peak - top)
        numer = numer + factor[:, :, None] * summed
        denom = denom + factor * total
    attn = (
        (numer / denom[:, :, None])
        .astype(jnp.bfloat16)
        .transpose(1, 0, 2)
        .reshape(count_of_rows, segment_width)
    )
    mixed = lax.psum_scatter(
        jnp.dot(attn, out_weight, preferred_element_type=jnp.float32).astype(jnp.bfloat16),
        "tp",
        scatter_dimension=0,
        tiled=True,
    )
    return mixed


def solution(mesh):
    return jax.shard_map(
        local,
        mesh=mesh,
        in_specs=(P("ctx", "tp"), P("ctx", "tp"), P("ctx", "tp"), P(), P("tp", None)),
        out_specs=P(("ctx", "tp"), None),
        check_vma=False,
    )
```

profile of v0, /device:TPU:1, one launch (start us, length us, event | category | flops | bytes accessed | tf_op | source)
XLA Modules:
  0.0 332.6 jit_solution(5016633176902496921)
XLA Ops:
  7.5 4.0 %reshape.280 = bf16[64,16,8,64]{3,2,1,0:T(8,128)(2,1)} reshape(bf16[1024,512]{1,0:T(8,128)(2,1)} %param.9) | data formatting | bytes 2097152 | tf_op jit(solution)/shard_map/reshape | solution.py:19
  11.4 3.9 %reshape.281 = bf16[64,16,8,64]{3,2,1,0:T(8,128)(2,1)} reshape(bf16[1024,512]{1,0:T(8,128)(2,1)} %param.10) | data formatting | bytes 2097152 | tf_op jit(solution)/shard_map/reshape | solution.py:19
  17.4 6.0 %select_reduce_fusion.2 = (bf16[64,8,64]{2,1,0:T(8,128)(2,1)}, bf16[64,8,64]{2,1,0:T(8,128)(2,1)S(1)}, bf16[64,8,64]{2,1,0:T(8,128)(2,1)S(1)}) fusion(bf16[64,16,8,64]{3,2,1,0:T(8,128)(2,1)} %reshape.280, pred[16,8]{1,0:T(8,128)(4,1)S(1)} %iota_compare_fusion, bf16[64,16,8,64]{3,2,1,0:T(8,128)(2,1)} %reshape.281, bf16[64,16,8,64]{3,2,1,0:T(8,128)(2,1)} %reshape.282), kind=kLoop, calls=%fused_computation.51 | loop fusion | flops 3047424 | bytes 3342464 | tf_op jit(solution)/shard_map/reduce_sum | solution.py:23
  26.8 3.9 %reshape.278 = bf16[128,8,8,64]{3,2,1,0:T(8,128)(2,1)} reshape(bf16[1024,512]{1,0:T(8,128)(2,1)} %param.10) | data formatting | bytes 2097152 | tf_op jit(solution)/shard_map/reshape | solution.py:19
  30.7 3.9 %reshape.279 = bf16[128,8,8,64]{3,2,1,0:T(8,128)(2,1)} reshape(bf16[1024,512]{1,0:T(8,128)(2,1)} %param.11) | data formatting | bytes 2097152 | tf_op jit(solution)/shard_map/reshape | solution.py:19
  34.6 6.4 %select_reduce_fusion.4 = (bf16[128,8,64]{2,1,0:T(8,128)(2,1)S(1)}, bf16[128,8,64]{2,1,0:T(8,128)(2,1)}, bf16[128,8,64]{2,1,0:T(8,128)(2,1)}) fusion(bf16[128,8,8,64]{3,2,1,0:T(8,128)(2,1)} %reshape.278, pred[8,8]{1,0:T(8,128)(4,1)S(1)} %get-tuple-element.179, bf16[128,8,8,64]{3,2,1,0:T(8,128)(2,1)} %reshape.279, bf16[128,8,8,64]{3,2,1,0:T(8,128)(2,1)} %reshape.277), kind=kLoop, calls=%fused_computation.53 | loop fusion | flops 2949120 | bytes 3539008 | tf_op jit(solution)/shard_map/reduce_sum | solution.py:23
  42.4 3.8 %collective-permute-start = (bf16[2,128,512]{1,2,0:T(8,128)(2,1)S(1)}, bf16[2,128,512]{1,2,0:T(8,128)(2,1)S(1)}, u32[]{:S(2)}, u32[]{:S(2)}) collective-permute-start(bf16[2,128,512]{1,2,0:T(8,128)(2,1)S(1)} %pad_maximum_fusion.3), channel_id=1, source_target_pairs={{0,4},{4,0},{8,12},{12,8},{16,20},{20,16},{24,28},{28,24},{32,36},... | collective-permute-start | bytes 786440 | tf_op jit(solution)/shard_map/ppermute | solution.py:14
  46.2 5.0 %collective-permute-done = bf16[2,128,512]{1,2,0:T(8,128)(2,1)S(1)} collective-permute-done((bf16[2,128,512]{1,2,0:T(8,128)(2,1)S(1)}, bf16[2,128,512]{1,2,0:T(8,128)(2,1)S(1)}, u32[]{:S(2)}, u32[]{:S(2)}) %collective-permute-start) | collective-permute-done | bytes 262176 | tf_op jit(solution)/shard_map/ppermute | solution.py:14
  60.4 7.5 %collective-permute-done.1 = bf16[2,256,512]{1,2,0:T(8,128)(2,1)} collective-permute-done((bf16[2,256,512]{1,2,0:T(8,128)(2,1)}, bf16[2,256,512]{1,2,0:T(8,128)(2,1)}, u32[]{:S(2)}, u32[]{:S(2)}) %collective-permute-start.1) | collective-permute-done | bytes 524320 | tf_op jit(solution)/shard_map/ppermute | solution.py:14
  70.0 3.2 collective-permute-start.2
  73.2 40.8 %while.30 = (s32[]{:T(128)}, f32[8,1024]{1,0:T(8,128)S(1)}, f32[8,1024]{1,0:T(8,128)S(1)}, f32[8,1024,64]{1,2,0:T(8,128)}, bf16[8,1024,64]{1,2,0:T(8,128)(2,1)},...) while((s32[]{:T(128)}, f32[8,1024]{1,0:T(8,128)S(1)}, f32[8,1024]{1,0:T(8,128)S(1)}, ...), condition=%wide.region_3.4_spmd.clone, body=%wide.region_0.3_spmd.sunk.clone | while | flops 276822016 | bytes 13273173 | solution.py:64
  85.1 2.5 fusion.78
  116.5 3.8 %copy.46 = f32[8,1024,64]{2,1,0:T(8,128)} copy(f32[8,1024,64]{1,2,0:T(8,128)} %get-tuple-element.85) | data formatting | bytes 4194304 | tf_op jit(solution)/shard_map/while | solution.py:64
  120.3 5.2 %collective-permute-done.2 = bf16[2,512,512]{1,2,0:T(8,128)(2,1)} collective-permute-done((bf16[2,512,512]{1,2,0:T(8,128)(2,1)}, bf16[2,512,512]{1,2,0:T(8,128)(2,1)}, u32[]{:S(2)}, u32[]{:S(2)}) %collective-permute-start.2) | collective-permute-done | bytes 1048608 | tf_op jit(solution)/shard_map/ppermute | solution.py:14
  128.3 19.4 %while.31 = (s32[]{:T(128)}, f32[8,128]{1,0:T(8,128)S(1)}, f32[8,128]{1,0:T(8,128)S(1)}, f32[8,128,64]{1,2,0:T(8,128)}, bf16[8,128,64]{2,1,0:T(8,128)(2,1)}, /*i...) while((s32[]{:T(128)}, f32[8,128]{1,0:T(8,128)S(1)}, f32[8,128]{1,0:T(8,128)S(1)}, ...), condition=%wide.region_10.11_spmd.clone, body=%wide.region_7.10_spmd.sunk.clone | while | flops 34340608 | bytes 1906773 | solution.py:79
  149.8 45.6 %all-gather.2.cloned.1.call-done = bf16[2,4096,512]{2,0,1:T(2,128)(2,1)} async-done(((bf16[2,64,512]{2,0,1:T(2,128)(2,1)}), bf16[2,4096,512]{2,0,1:T(2,128)(2,1)}) %all-gather.2.cloned.1.call-update) | async-done | bytes 8388624 | tf_op jit(solution)/shard_map/all_gather | solution.py:104
  195.4 17.1 %fusion.51 = (bf16[1,4096,512]{2,0,1:T(2,128)(2,1)}, bf16[1,4096,512]{2,0,1:T(2,128)(2,1)}) fusion(bf16[2,4096,512]{2,0,1:T(2,128)(2,1)} %all-gather.2.cloned.1.call-done), kind=kLoop, calls=%fused_computation.82 | loop fusion | bytes 16777216 | tf_op jit(solution)/shard_map/slice | solution.py:107
  212.5 18.5 %copy.44 = bf16[1,4096,512]{1,2,0:T(8,128)(2,1)} copy(bf16[1,4096,512]{2,0,1:T(2,128)(2,1)} %get-tuple-element.174) | data formatting | bytes 8388608 | tf_op jit(solution)/shard_map/slice | solution.py:106
  231.0 3.5 %multiply_reduce_fusion.1 = (f32[8,64]{1,0:T(8,128)S(1)}, f32[8,64,4096]{2,1,0:T(8,128)S(1)}) fusion(bf16[8,4096,64]{1,2,0:T(8,128)(2,1)} %bitcast.134, bf16[8,64,64]{2,0,1:T(8,128)(2,1)S(1)} %bitcast.153), kind=kOutput, calls=%fused_computation.33 | convolution fusion | flops 272629248 | bytes 12650496 | tf_op jit(solution)/shard_map/hld,hsd->hls/dot_general | solution.py:108
  238.3 18.4 %copy.48 = bf16[1,4096,512]{1,2,0:T(8,128)(2,1)} copy(bf16[1,4096,512]{2,0,1:T(2,128)(2,1)} %get-tuple-element.173) | data formatting | bytes 8388608 | tf_op jit(solution)/shard_map/slice | solution.py:107
  256.7 6.3 %fusion.35 = f32[8,64,64]{2,1,0:T(8,128)S(1)} fusion(bf16[8,4096,64]{1,2,0:T(8,128)(2,1)} %bitcast.135, f32[8,64,4096]{2,1,0:T(8,128)} %copy-done.1, f32[8,64]{1,0:T(8,128)S(1)} %broadcast_maximum_fusion), kind=kOutput, calls=%fused_computation.36 | convolution fusion | flops 274726912 | bytes 12716032 | tf_op jit(solution)/shard_map/hls,hsd->hld/dot_general | solution.py:114
  263.1 8.9 %fusion.44 = bf16[8,1024,64]{2,1,0:T(8,128)(2,1)} fusion(f32[8,1024,64]{2,1,0:T(8,128)S(1)} %copy-done.2, f32[8,1024]{1,0:T(8,128)S(1)} %get-tuple-element.165, f32[8,64,64]{2,1,0:T(8,128)S(1)} %fusion.35, f32[8,1024]{1,0:T(8,128)S(1)} %get-tuple-element.168, f32[8,128,64]{2,1,0:T(8,128)S(1)} %copy.47, f32[8,1024]{1,0:T(8,128)S(1)} %get-tuple-element.167, ...), kind=kLoop, calls=%fused_computation.46 | loop fusion | flops 4718592 | bytes 3686400 | tf_op jit(solution)/shard_map/convert_element_type | solution.py:136
  273.9 4.3 %convolution_convert_fusion = bf16[1024,2048]{1,0:T(8,128)(2,1)} fusion(bf16[1024,512]{0,1:T(8,128)(2,1)S(1)} %bitcast.151, bf16[512,2048]{1,0:T(8,128)(2,1)S(1)} %copy-done), kind=kOutput, calls=%fused_computation.47 | convolution fusion | flops 2149580800 | bytes 7340032 | tf_op jit(solution)/shard_map/dot_general | solution.py:141
  278.3 47.5 %reduce-scatter.2.cloned.1.call-done = bf16[256,2048]{1,0:T(8,128)(2,1)} async-done(((bf16[1024,2048]{1,0:T(8,128)(2,1)}), bf16[256,2048]{1,0:T(8,128)(2,1)}) %reduce-scatter.2.cloned.1.call-update) | async-done | bytes 1048592 | tf_op jit(solution)/shard_map/reduce_scatter | solution.py:140
  (144 shorter events, 89.4 us)
Async XLA Ops:
  6.5 267.4 %copy-start = (bf16[512,2048]{1,0:T(8,128)(2,1)S(1)}, bf16[512,2048]{1,0:T(8,128)(2,1)}, u32[]{:S(2)}) copy-start(bf16[512,2048]{1,0:T(8,128)(2,1)} %param.13) | copy-start | bytes 6291460
  6.5 8.8 %copy-start.4 = (bf16[1024,512]{1,0:T(8,128)(2,1)S(1)}, bf16[1024,512]{1,0:T(8,128)(2,1)}, u32[]{:S(2)}) copy-start(bf16[1024,512]{1,0:T(8,128)(2,1)} %param.11) | copy-start | bytes 3145732
  6.5 188.8 %all-gather.2.cloned.1.call-start = ((), (), s32[]{:S(2)}) async-start(), calls=%async_computation.1 | async-start | bytes 8519680 | tf_op jit(solution)/shard_map/all_gather | solution.py:104
  17.4 7.3 %copy-start.3 = (bf16[1024,512]{1,0:T(8,128)(2,1)S(1)}, bf16[1024,512]{1,0:T(8,128)(2,1)}, u32[]{:S(2)}) copy-start(bf16[1024,512]{1,0:T(8,128)(2,1)} %param.9) | copy-start | bytes 3145732
  24.6 301.1 %reduce-scatter.2.cloned.1.call-start = ((), (), s32[]{:S(2)}) async-start(), calls=%async_computation.2 | async-start | bytes 5242880 | tf_op jit(solution)/shard_map/reduce_scatter | solution.py:140
  42.4 8.8 %collective-permute-start = (bf16[2,128,512]{1,2,0:T(8,128)(2,1)S(1)}, bf16[2,128,512]{1,2,0:T(8,128)(2,1)S(1)}, u32[]{:S(2)}, u32[]{:S(2)}) collective-permute-start(bf16[2,128,512]{1,2,0:T(8,128)(2,1)S(1)} %pad_maximum_fusion.3), channel_id=1, source_target_pairs={{0,4},{4,0},{8,12},{12,8},{16,20},{20,16},{24,28},{28,24},{32,36},... | collective-permute-start | bytes 786440 | tf_op jit(solution)/shard_map/ppermute | solution.py:14
  51.2 0.7 copy-start.5
  52.8 15.0 %collective-permute-start.1 = (bf16[2,256,512]{1,2,0:T(8,128)(2,1)}, bf16[2,256,512]{1,2,0:T(8,128)(2,1)}, u32[]{:S(2)}, u32[]{:S(2)}) collective-permute-start(bf16[2,256,512]{1,2,0:T(8,128)(2,1)} %pad_maximum_fusion.2), channel_id=1, source_target_pairs={{0,8},{4,12},{8,0},{12,4},{16,24},{20,28},{24,16},{28,20},{32,40},... | collective-permute-start | bytes 1572872 | tf_op jit(solution)/shard_map/ppermute | solution.py:14
  70.0 55.5 %collective-permute-start.2 = (bf16[2,512,512]{1,2,0:T(8,128)(2,1)}, bf16[2,512,512]{1,2,0:T(8,128)(2,1)}, u32[]{:S(2)}, u32[]{:S(2)}) collective-permute-start(bf16[2,512,512]{1,2,0:T(8,128)(2,1)} %pad_maximum_fusion.1), channel_id=1, source_target_pairs={{0,16},{4,20},{8,24},{12,28},{16,0},{20,4},{24,8},{28,12},{32,48},... | collective-permute-start | bytes 3145736 | tf_op jit(solution)/shard_map/ppermute | solution.py:14
  114.1 11.4 %copy-start.6 = (bf16[2,128,512]{1,2,0:T(8,128)(2,1)S(1)}, bf16[2,128,512]{1,2,0:T(8,128)(2,1)}, u32[]{:S(2)}) copy-start(bf16[2,128,512]{1,2,0:T(8,128)(2,1)} %copy-done.5) | copy-start | bytes 786436
  212.5 18.5 %copy-start.7 = (bf16[64,8,64]{2,1,0:T(8,128)(2,1)S(1)}, bf16[64,8,64]{2,1,0:T(8,128)(2,1)}, u32[]{:S(2)}) copy-start(bf16[64,8,64]{2,1,0:T(8,128)(2,1)} %get-tuple-element.131) | copy-start | bytes 196612
  234.5 3.2 copy-start.1
  256.7 6.3 %copy-start.2 = (f32[8,1024,64]{2,1,0:T(8,128)S(1)}, f32[8,1024,64]{2,1,0:T(8,128)}, u32[]{:S(2)}) copy-start(f32[8,1024,64]{2,1,0:T(8,128)} %copy.46) | copy-start | bytes 6291460
Sparse Core Ops, SparseCore 0:
  24.8 170.5 all-gather.1
  278.4 47.2 reduce-scatter.1
where the time goes:
time: 334 us; the launch traced here: 333 us
  waiting for transfers between devices  111 us (33%)
  local copies, waits for them, and re-layouts  97.9 us (29%)
  matrix products  64 us (19%)
  other arithmetic  36.3 us (11%)
  between operations  13.6 us (4%)
  starting transfers between devices  9.53 us (3%)
    reduce_scatter x1, waiting for transfers between devices, local(): lax.psum_scatter(jnp.dot(attn, out_weight, preferred_element_type=jnp.flo...  47.5 us
    all_gather x1, waiting for transfers between devices, local(): piece = lax.all_gather(far_kv, 'ctx', axis=1, tiled=True)  45.6 us
    slice x2, local copies, waits for them, and re-layouts, local(): piece_v = heads_first(piece[1])  35.5 us
    dot_general x16, matrix products, attend(): jnp.dot(expo.astype(jnp.bfloat16), value_per_head, preferred_element_type...  26.9 us
    dot_general x16, matrix products, attend(): jnp.dot(query_per_head, key_per_head.T, preferred_element_type=jnp.float32)  23.1 us
    reshape x6, local copies, waits for them, and re-layouts, select_rows(): field.reshape(count_of_rows // dilation, dilation, heads_on_shard, HEAD_DIM)  19.8 us
    slice x1, local copies, waits for them, and re-layouts, local(): piece_k = heads_first(piece[0])  18.5 us
    ppermute x3, waiting for transfers between devices, partner_2(): lax.ppermute(shard, axis, [(i, i ^ 1 << stride) for i in range(lax.axis_s...  17.6 us
  transfers between devices with their start and end apart: 5, of which 5 were waited for; matrix products, arithmetic and copies ran while one was open for 29% of the time, Pallas kernels for 0%

commit v1 on v0

--- a/solution.py
+++ b/solution.py
@@ -101,7 +101,9 @@
         ]
     )
     far_rows = distant_query.shape[1]
-    piece = lax.all_gather(far_kv, "ctx", axis=1, tiled=True)
+    piece = jnp.concatenate(
+        lax.all_to_all(jnp.stack([far_kv] * lax.axis_size("ctx")), "ctx", 0, 0), axis=1
+    )
     fold_peak = jnp.full((heads_on_shard, far_rows), NEG, jnp.float32)
     piece_k = heads_first(piece[0])
     piece_v = heads_first(piece[1])

time: 334 us -> 442 us (1.32)
  waiting for transfers between devices: 111 us -> 214 us
  starting transfers between devices: 9.53 us -> 22.1 us
  matrix products: 64 us -> 59.2 us
    ppermute x3, waiting for transfers between devices: 17.6 us -> 163 us  [partner_2(): lax.ppermute(shard, axis, [(i, i ^ 1 << stride) for i in range(lax.axis_s...]
    another operation x0 -> x5, local copies, waits for them, and re-layouts: none -> 46.2 us  [the longest x4 41.9 us: heads_first(): field.reshape(field.shape[0], heads_on_shard, HEAD_DIM).transpose(1, 0, 2)]
    all_gather x1 -> x0, waiting for transfers between devices: 45.6 us -> none  [local(): piece = lax.all_gather(far_kv, 'ctx', axis=1, tiled=True)]
    slice x2 -> x1, local copies, waits for them, and re-layouts: 35.5 us -> 5.96 us  [local(): piece_v = heads_first(piece[1])]
    slice x1 -> x0, local copies, waits for them, and re-layouts: 18.5 us -> none  [local(): piece_k = heads_first(piece[0])]
    all_to_all x0 -> x1, starting transfers between devices: none -> 15.5 us  [local(): lax.all_to_all(jnp.stack([far_kv] * lax.axis_size('ctx')), 'ctx', 0, 0)]
    dot_general x1, matrix products: 6.28 us -> 1.58 us  [local(): jnp.einsum('hls,hsd->hld', expo.astype(jnp.bfloat16), piece_v, preferred_...]
  transfers between devices with their start and end apart: 5 -> 5, of which waited for: 5 -> 3; matrix products, arithmetic and copies ran while one was open for 29% -> 22% of each run, Pallas kernels for 0% -> 0%
where the time goes in v1:
time: 442 us; the launch traced here: 440 us
  waiting for transfers between devices  214 us (48%)
  local copies, waits for them, and re-layouts  94.6 us (21%)
  matrix products  59.2 us (13%)
  other arithmetic  36.4 us (8%)
  starting transfers between devices  22.1 us (5%)
  between operations  13.6 us (3%)
    ppermute x3, waiting for transfers between devices, partner_2(): lax.ppermute(shard, axis, [(i, i ^ 1 << stride) for i in range(lax.axis_s...  163 us
    reduce_scatter x1, waiting for transfers between devices, local(): lax.psum_scatter(jnp.dot(attn, out_weight, preferred_element_type=jnp.flo...  51.2 us
    another operation x4, local copies, waits for them, and re-layouts, heads_first(): field.reshape(field.shape[0], heads_on_shard, HEAD_DIM).transpose(1, 0, 2)  41.9 us
    dot_general x16, matrix products, attend(): jnp.dot(expo.astype(jnp.bfloat16), value_per_head, preferred_element_type...  26.8 us
    dot_general x16, matrix products, attend(): jnp.dot(query_per_head, key_per_head.T, preferred_element_type=jnp.float32)  23.1 us
    reshape x6, local copies, waits for them, and re-layouts, select_rows(): field.reshape(count_of_rows // dilation, dilation, heads_on_shard, HEAD_DIM)  19.9 us
    all_to_all x1, starting transfers between devices, local(): lax.all_to_all(jnp.stack([far_kv] * lax.axis_size('ctx')), 'ctx', 0, 0)  15.5 us
    reduce_sum x2, other arithmetic, select_rows(): return jnp.sum(jnp.where(picked, shaped, jnp.zeros_like(shaped)), axis=1)  12.3 us
  transfers between devices with their start and end apart: 5, of which 3 were waited for; matrix products, arithmetic and copies ran while one was open for 22% of the time, Pallas kernels for 0%

profile of v1, /device:TPU:1, one launch (start us, length us, event | category | flops | bytes accessed | tf_op | source)
XLA Modules:
  0.0 440.3 jit_solution(14819962510180356459)
XLA Ops:
  7.5 4.0 reshape.290
  11.4 3.9 reshape.291
  17.4 5.9 %select_reduce_fusion.2 = (bf16[64,8,64]{2,1,0:T(8,128)(2,1)}, bf16[64,8,64]{2,1,0:T(8,128)(2,1)S(1)}, bf16[64,8,64]{2,1,0:T(8,128)(2,1)S(1)}) fusion(bf16[64,16,8,64]{3,2,1,0:T(8,128)(2,1)} %reshape.290, pred[16,8]{1,0:T(8,128)(4,1)S(1)} %iota_compare_fusion, bf16[64,16,8,64]{3,2,1,0:T(8,128)(2,1)} %reshape.291, bf16[64,16,8,64]{3,2,1,0:T(8,128)(2,1)} %reshape.292), kind=kLoop, calls=%fused_computation.54 | loop fusion | flops 3047424 | bytes 3342464 | tf_op jit(solution)/shard_map/reduce_sum | solution.py:23
  23.7 4.3 stack.8
  27.9 15.5 %all-to-all-start = ((bf16[64,2,64,512]{3,2,1,0:T(8,128)(2,1)}), bf16[64,2,64,512]{3,2,1,0:T(8,128)(2,1)}, u32[]{:S(2)}, u32[]{:S(2)}) async-start(bf16[64,2,64,512]{3,2,1,0:T(8,128)(2,1)} %stack.8), calls=%async_computation | async-start | bytes 16777216 | tf_op jit(solution)/shard_map/all_to_all | solution.py:105
  45.8 3.9 reshape.288
  49.7 3.9 reshape.289
  53.7 6.4 %select_reduce_fusion.4 = (bf16[128,8,64]{2,1,0:T(8,128)(2,1)S(1)}, bf16[128,8,64]{2,1,0:T(8,128)(2,1)}, bf16[128,8,64]{2,1,0:T(8,128)(2,1)}) fusion(bf16[128,8,8,64]{3,2,1,0:T(8,128)(2,1)} %reshape.288, pred[8,8]{1,0:T(8,128)(4,1)S(1)} %get-tuple-element.179, bf16[128,8,8,64]{3,2,1,0:T(8,128)(2,1)} %reshape.289, bf16[128,8,8,64]{3,2,1,0:T(8,128)(2,1)} %reshape.287), kind=kLoop, calls=%fused_computation.56 | loop fusion | flops 2949120 | bytes 3539008 | tf_op jit(solution)/shard_map/reduce_sum | solution.py:23
  61.5 2.5 collective-permute-start
  64.0 9.0 %collective-permute-done = bf16[2,128,512]{1,2,0:T(8,128)(2,1)S(1)} collective-permute-done((bf16[2,128,512]{1,2,0:T(8,128)(2,1)S(1)}, bf16[2,128,512]{1,2,0:T(8,128)(2,1)S(1)}, u32[]{:S(2)}, u32[]{:S(2)}) %collective-permute-start) | collective-permute-done | bytes 262176 | tf_op jit(solution)/shard_map/ppermute | solution.py:14
  81.8 153.6 %collective-permute-done.1 = bf16[2,256,512]{1,2,0:T(8,128)(2,1)} collective-permute-done((bf16[2,256,512]{1,2,0:T(8,128)(2,1)}, bf16[2,256,512]{1,2,0:T(8,128)(2,1)}, u32[]{:S(2)}, u32[]{:S(2)}) %collective-permute-start.1) | collective-permute-done | bytes 524320 | tf_op jit(solution)/shard_map/ppermute | solution.py:14
  239.3 40.5 %while.30 = (s32[]{:T(128)}, f32[8,1024]{1,0:T(8,128)S(1)}, f32[8,1024]{1,0:T(8,128)S(1)}, f32[8,1024,64]{1,2,0:T(8,128)}, bf16[8,1024,64]{1,2,0:T(8,128)(2,1)},...) while((s32[]{:T(128)}, f32[8,1024]{1,0:T(8,128)S(1)}, f32[8,1024]{1,0:T(8,128)S(1)}, ...), condition=%wide.region_3.4_spmd.clone, body=%wide.region_0.3_spmd.sunk.clone | while | flops 276822016 | bytes 13273181 | solution.py:64
  256.9 2.5 fusion.78
  282.2 3.8 copy.48
  288.7 19.4 %while.31 = (s32[]{:T(128)}, f32[8,128]{1,0:T(8,128)S(1)}, f32[8,128]{1,0:T(8,128)S(1)}, f32[8,128,64]{1,2,0:T(8,128)}, bf16[8,128,64]{2,1,0:T(8,128)(2,1)}, /*i...) while((s32[]{:T(128)}, f32[8,128]{1,0:T(8,128)S(1)}, f32[8,128]{1,0:T(8,128)S(1)}, ...), condition=%wide.region_10.11_spmd.clone, body=%wide.region_7.10_spmd.sunk.clone | while | flops 34340608 | bytes 1906781 | solution.py:79
  310.2 6.0 %fusion.53 = (bf16[1,64,64,512]{3,2,0,1:T(8,128)(2,1)}, bf16[1,64,64,512]{3,2,0,1:T(8,128)(2,1)}) fusion(bf16[2,64,64,512]{3,2,0,1:T(8,128)(2,1)} %bitcast.28), kind=kLoop, calls=%fused_computation.84 | loop fusion | bytes 16777216 | tf_op jit(solution)/shard_map/slice | solution.py:109
  316.2 11.2 %reshape_squeeze.15 = bf16[4096,8,64]{2,1,0:T(8,128)(2,1)} reshape(bf16[1,64,64,512]{3,2,0,1:T(8,128)(2,1)} %get-tuple-element.173) | data formatting | bytes 8388608 | tf_op jit(solution)/shard_map/reshape;squeeze | solution.py:62
  327.3 9.8 %copy.50 = bf16[4096,8,64]{0,2,1:T(8,128)(2,1)} copy(bf16[4096,8,64]{2,1,0:T(8,128)(2,1)} %reshape_squeeze.15) | data formatting | bytes 8388608 | tf_op jit(solution)/shard_map/reshape;squeeze | solution.py:62
  337.1 11.2 %reshape_squeeze.14 = bf16[4096,8,64]{2,1,0:T(8,128)(2,1)} reshape(bf16[1,64,64,512]{3,2,0,1:T(8,128)(2,1)} %get-tuple-element.174) | data formatting | bytes 8388608 | tf_op jit(solution)/shard_map/reshape;squeeze | solution.py:62
  348.3 9.8 %copy.46 = bf16[4096,8,64]{0,2,1:T(8,128)(2,1)} copy(bf16[4096,8,64]{2,1,0:T(8,128)(2,1)} %reshape_squeeze.14) | data formatting | bytes 8388608 | tf_op jit(solution)/shard_map/reshape;squeeze | solution.py:62
  358.1 3.5 multiply_reduce_fusion.1
  366.0 9.9 %fusion.47 = bf16[8,1024,64]{2,1,0:T(8,128)(2,1)} fusion(f32[8,1024,64]{2,1,0:T(8,128)} %copy.48, f32[8,1024]{1,0:T(8,128)S(1)} %get-tuple-element.165, f32[8,64,64]{2,1,0:T(8,128)S(1)} %fusion.35, f32[8,1024]{1,0:T(8,128)S(1)} %get-tuple-element.168, f32[8,128,64]{2,1,0:T(8,128)S(1)} %copy.49, f32[8,1024]{1,0:T(8,128)S(1)} %get-tuple-element.167, ...), kind=kLoop, calls=%fused_computation.49 | loop fusion | flops 4718592 | bytes 3686400 | tf_op jit(solution)/shard_map/convert_element_type | solution.py:138
  377.9 4.3 convolution_convert_fusion
  382.2 51.2 %reduce-scatter.2.cloned.1.call-done = bf16[256,2048]{1,0:T(8,128)(2,1)} async-done(((bf16[1024,2048]{1,0:T(8,128)(2,1)}), bf16[256,2048]{1,0:T(8,128)(2,1)}) %reduce-scatter.2.cloned.1.call-update) | async-done | bytes 1048592 | tf_op jit(solution)/shard_map/reduce_scatter | solution.py:142
  (144 shorter events, 90.2 us)
Async XLA Ops:
  6.5 371.3 %copy-start = (bf16[512,2048]{1,0:T(8,128)(2,1)S(1)}, bf16[512,2048]{1,0:T(8,128)(2,1)}, u32[]{:S(2)}) copy-start(bf16[512,2048]{1,0:T(8,128)(2,1)} %param.13) | copy-start | bytes 6291460
  6.5 8.8 %copy-start.3 = (bf16[1024,512]{1,0:T(8,128)(2,1)S(1)}, bf16[1024,512]{1,0:T(8,128)(2,1)}, u32[]{:S(2)}) copy-start(bf16[1024,512]{1,0:T(8,128)(2,1)} %param.11) | copy-start | bytes 3145732
  27.9 15.8 %copy-start.2 = (bf16[1024,512]{1,0:T(8,128)(2,1)S(1)}, bf16[1024,512]{1,0:T(8,128)(2,1)}, u32[]{:S(2)}) copy-start(bf16[1024,512]{1,0:T(8,128)(2,1)} %param.9) | copy-start | bytes 3145732
  27.9 282.3 %all-to-all-start = ((bf16[64,2,64,512]{3,2,1,0:T(8,128)(2,1)}), bf16[64,2,64,512]{3,2,1,0:T(8,128)(2,1)}, u32[]{:S(2)}, u32[]{:S(2)}) async-start(bf16[64,2,64,512]{3,2,1,0:T(8,128)(2,1)} %stack.8), calls=%async_computation | async-start | bytes 16777216 | tf_op jit(solution)/shard_map/all_to_all | solution.py:105
  43.4 390.0 %reduce-scatter.2.cloned.1.call-start = ((), (), s32[]{:S(2)}) async-start(), calls=%async_computation.2 | async-start | bytes 5242880 | tf_op jit(solution)/shard_map/reduce_scatter | solution.py:142
  61.5 11.5 %collective-permute-start = (bf16[2,128,512]{1,2,0:T(8,128)(2,1)S(1)}, bf16[2,128,512]{1,2,0:T(8,128)(2,1)S(1)}, u32[]{:S(2)}, u32[]{:S(2)}) collective-permute-start(bf16[2,128,512]{1,2,0:T(8,128)(2,1)S(1)} %pad_maximum_fusion.3), channel_id=1, source_target_pairs={{0,4},{4,0},{8,12},{12,8},{16,20},{20,16},{24,28},{28,24},{32,36},... | collective-permute-start | bytes 786440 | tf_op jit(solution)/shard_map/ppermute | solution.py:14
  73.0 0.7 copy-start.4
  74.6 160.8 %collective-permute-start.1 = (bf16[2,256,512]{1,2,0:T(8,128)(2,1)}, bf16[2,256,512]{1,2,0:T(8,128)(2,1)}, u32[]{:S(2)}, u32[]{:S(2)}) collective-permute-start(bf16[2,256,512]{1,2,0:T(8,128)(2,1)} %pad_maximum_fusion.2), channel_id=1, source_target_pairs={{0,8},{4,12},{8,0},{12,4},{16,24},{20,28},{24,16},{28,20},{32,40},... | collective-permute-start | bytes 1572872 | tf_op jit(solution)/shard_map/ppermute | solution.py:14
  237.6 48.4 %collective-permute-start.2 = (bf16[2,512,512]{1,2,0:T(8,128)(2,1)}, bf16[2,512,512]{1,2,0:T(8,128)(2,1)}, u32[]{:S(2)}, u32[]{:S(2)}) collective-permute-start(bf16[2,512,512]{1,2,0:T(8,128)(2,1)} %pad_maximum_fusion.1), channel_id=1, source_target_pairs={{0,16},{4,20},{8,24},{12,28},{16,0},{20,4},{24,8},{28,12},{32,48},... | collective-permute-start | bytes 3145736 | tf_op jit(solution)/shard_map/ppermute | solution.py:14
  279.8 6.2 %copy-start.5 = (bf16[2,128,512]{1,2,0:T(8,128)(2,1)S(1)}, bf16[2,128,512]{1,2,0:T(8,128)(2,1)}, u32[]{:S(2)}) copy-start(bf16[2,128,512]{1,2,0:T(8,128)(2,1)} %copy-done.4) | copy-start | bytes 786436
  348.3 9.8 %copy-start.6 = (bf16[64,8,64]{2,1,0:T(8,128)(2,1)S(1)}, bf16[64,8,64]{2,1,0:T(8,128)(2,1)}, u32[]{:S(2)}) copy-start(bf16[64,8,64]{2,1,0:T(8,128)(2,1)} %get-tuple-element.131) | copy-start | bytes 196612
  361.6 2.2 copy-start.1
Sparse Core Ops, SparseCore 0:
  382.3 51.0 reduce-scatter.1
